TPU v7x, 32 devices: a whole 2x2x4 slice. The times are simulated.
32 devices in a mesh: groups: 2 (over y), pipe: 4 (over z), hour: 2 (over x), seg: 2 (over core).
Axes of the slice: x: 2, y: 2, z: 4, core: 2. Of those that a mesh axis runs over, the one named last changes fastest.
Arguments:
- segment_flow: float32 [16, 64, 1024], P(('groups', 'hour'), 'seg', 'pipe'), parts along dimension 0, may hold values from -4 to 4
- linepack: float32 [16, 64, 1024], P(('groups', 'hour'), 'seg', 'pipe'), parts along dimension 0, may hold values from 0.2 to 2.4
- mass_dual: float32 [16, 64, 1024], P(('groups', 'hour'), 'seg', 'pipe'), parts along dimension 0, may hold values from -3 to 3
- momentum_dual: float32 [16, 64, 1024], P(('groups', 'hour'), 'seg', 'pipe'), parts along dimension 0, may hold values from -3 to 3
- contract_dual: float32 [16, 2, 32, 128], P(('groups', 'hour'), 'seg', 'pipe'), parts along dimension 0, may hold values from -3 to 3
- flow_cost: float32 [16, 64, 1024], P(('groups', 'hour'), 'seg', 'pipe'), parts along dimension 0, may hold values from -24 to 24
- injection: float32 [16, 64, 1024], P(('groups', 'hour'), 'seg', 'pipe'), parts along dimension 0, may hold values from -3 to 3
- contract_target: float32 [16, 2, 32, 128], P(('groups', 'hour'), 'seg', 'pipe'), parts along dimension 0, may hold values from 0.4 to 2
- friction_table: float32 [16], replicated, may hold values from 0.3 to 3
- friction_class: int32 [64, 2048], P('seg', ('groups', 'pipe')), parts along dimension 1, may hold values from 0 to 15
- matching: int32 [2048], P('groups'), parts along dimension 0, may hold values from 0 to 1023, as said below
- contract_map: int32 [16, 1024], P(('groups', 'hour')), parts along dimension 0, may hold values from 0 to 127
Outputs:
- flow_final: float32 [16, 64, 1024], P(('groups', 'hour'), 'seg', 'pipe'), parts along dimension 0
- linepack_final: float32 [16, 64, 1024], P(('groups', 'hour'), 'seg', 'pipe'), parts along dimension 0
- mass_dual_final: float32 [16, 64, 1024], P(('groups', 'hour'), 'seg', 'pipe'), parts along dimension 0
- momentum_dual_final: float32 [16, 64, 1024], P(('groups', 'hour'), 'seg', 'pipe'), parts along dimension 0
- contract_dual_final: float32 [16, 2, 32, 128], P(('groups', 'hour'), 'seg', 'pipe'), parts along dimension 0
- primal_weight: float32 [2], P('groups'), parts along dimension 0
There are 2 independent parts, one for each index of `groups`. A program takes and returns all parts, laid end to end along the dimension named above; an argument that names none is the same for every part. Nothing has to cross between parts.
Inputs may be any that keep to these rules, and one draw needn't show every extreme that they name: `matching`: every pipe's inlet is fed by the outlet of exactly one pipe: each number of 0 to 1023 appears once; for any two blocks of 256 consecutive pipes, exactly 64 pipes of the first are fed from outlets of the second.
All inputs are finite; a program needn't handle non-finite values.
Results may differ from a plain program's by a relative error of at most 0.0001.
Values sent between devices are 32-bit elements; how exact they have to be, the bound alone decides.
A program may use at most 64 MiB of HBM per device.

v0:
```python
import math
import jax
import jax.numpy as jnp
from jax import lax
from jax.sharding import PartitionSpec as P

ITERS = 2
FLOW_CAP = 1.5
PACK_CAP = 2.5
STEP_SCALE = 0.25
NORM_EPS = 1e-06


def padded(cells, sides, width):
    for axis, dim in sides:
        count = lax.axis_size(axis)
        ends = count - 1
        head = lax.slice_in_dim(cells, 0, width, axis=dim)
        tail = lax.slice_in_dim(cells, cells.shape[dim] - width, cells.shape[dim], axis=dim)
        cells = jnp.concatenate(
            [
                lax.ppermute(tail, axis, [(i, (i + 1) % count) for i in range(ends)]),
                cells,
                lax.ppermute(head, axis, [((i + 1) % count, i) for i in range(ends)]),
            ],
            axis=dim,
        )
    return cells


def widened_pair(stacked):
    return padded(stacked, (("hour", 1), ("seg", 2)), 1)


def other_half(edge_row, half_index, partner_local):
    gathered = lax.all_gather(edge_row[:, None, :], ("pipe", "seg"), axis=1, tiled=True)
    hour_rows, row_count, row_width = gathered.shape
    seg_count = lax.axis_size("seg")
    picked = gathered.reshape(hour_rows, row_count // seg_count, seg_count, row_width)[
        :, :, half_index, :
    ]
    far_rows = picked.reshape(hour_rows, row_count // seg_count * row_width)
    return jnp.take(far_rows, partner_local, axis=1)


def contract_local(values, contract_rows, class_count):
    hour_rows, seg_rows, pipe_rows = values.shape
    block = math.gcd(pipe_rows, 2048)
    classes = jnp.arange(class_count, dtype=jnp.int32)

    def add_block(block_index, total):
        partial_value = lax.dynamic_slice_in_dim(values, block_index * block, block, 2)
        row_map = lax.dynamic_slice_in_dim(contract_rows, block_index * block, block, 1)
        onehot = (row_map[:, :, None] == classes[None, None, :]).astype(jnp.float32)
        return total + jnp.einsum(
            "hsp,hpc->hsc",
            partial_value,
            onehot,
            precision=lax.Precision.HIGHEST,
            preferred_element_type=jnp.float32,
        )

    return lax.fori_loop(
        0, pipe_rows // block, add_block, jnp.zeros((hour_rows, seg_rows, class_count), jnp.float32)
    )


def spread_local(duals, contract_rows):
    hour_rows, seg_rows, class_count = duals.shape
    pipe_rows = contract_rows.shape[1]
    block = math.gcd(pipe_rows, 2048)
    classes = jnp.arange(class_count, dtype=jnp.int32)

    def fill_block(block_index, result_now):
        row_map = lax.dynamic_slice_in_dim(contract_rows, block_index * block, block, 1)
        onehot = (row_map[:, :, None] == classes[None, None, :]).astype(jnp.float32)
        partial_value = jnp.einsum(
            "hsc,hpc->hsp",
            duals,
            onehot,
            precision=lax.Precision.HIGHEST,
            preferred_element_type=jnp.float32,
        )
        return lax.dynamic_update_slice_in_dim(result_now, partial_value, block_index * block, 2)

    return lax.fori_loop(
        0, pipe_rows // block, fill_block, jnp.zeros((hour_rows, seg_rows, pipe_rows), jnp.float32)
    )


def on_device(
    segment_flow,
    linepack,
    mass_dual,
    momentum_dual,
    contract_dual,
    flow_cost,
    injection,
    contract_target,
    friction_table,
    friction_class,
    matching,
    contract_map,
):
    hour_rows, seg_rows, pipe_rows = segment_flow.shape
    class_count = contract_dual.shape[3]
    pipe_count = lax.axis_size("pipe")
    total_pipes = pipe_rows * pipe_count
    share_scale = class_count / total_pipes
    pipe_start = lax.axis_index("pipe") * pipe_rows
    seg_index = lax.axis_index("seg")
    at_start = seg_index == 0
    at_end = seg_index == lax.axis_size("seg") - 1
    levels = jnp.arange(friction_table.shape[0], dtype=jnp.int32)
    friction = jnp.sum(
        jnp.where(
            friction_class[None] == levels[:, None, None], friction_table[:, None, None], 0.0
        ),
        axis=0,
    )[None]
    inverse = (
        jnp.zeros_like(matching).at[matching].set(jnp.arange(matching.shape[0], dtype=jnp.int32))
    )
    source_local = lax.dynamic_slice_in_dim(matching, pipe_start, pipe_rows)
    target_local = lax.dynamic_slice_in_dim(inverse, pipe_start, pipe_rows)
    contract_now = contract_dual.reshape(hour_rows, contract_dual.shape[2], class_count)
    target_now = contract_target.reshape(hour_rows, contract_target.shape[2], class_count)
    weight = jnp.float32(1.0)
    for iteration in range(ITERS):
        primal_step = STEP_SCALE / weight
        dual_step = STEP_SCALE * weight
        widened = widened_pair(jnp.stack([mass_dual, momentum_dual]))
        last_base = widened[0, 1:-1, -1, :]
        later_hour = widened[0, 2:, 1:-1, :]
        before_seg = widened[1, 1:-1, :-2, :]
        returned = other_half(mass_dual[:, 0, :], 0, target_local)
        last_row = last_base + jnp.where(at_end, returned, 0.0)
        next_seg = jnp.concatenate([mass_dual[:, 1:, :], last_row[:, None, :]], axis=1)
        grad_flow = mass_dual - next_seg + friction * momentum_dual
        hour_spread = spread_local(contract_now, contract_map)
        spread = lax.all_to_all(hour_spread, "pipe", split_axis=2, concat_axis=1, tiled=True)
        grad_pack = mass_dual - later_hour - momentum_dual + before_seg + share_scale * spread
        grad_flow, grad_pack = (grad_flow, grad_pack)
        flow_next = jnp.clip(
            segment_flow - primal_step * (flow_cost - grad_flow), -FLOW_CAP, FLOW_CAP
        )
        pack_next = jnp.clip(linepack + primal_step * grad_pack, 0.0, PACK_CAP)
        flow_bar = 2.0 * flow_next - segment_flow
        pack_bar = 2.0 * pack_next - linepack
        forward_widened = widened_pair(jnp.stack([flow_bar, pack_bar]))
        first_base = forward_widened[0, 1:-1, 0, :]
        earlier = forward_widened[1, :-2, 1:-1, :]
        after_seg = forward_widened[1, 1:-1, 2:, :]
        inflow = other_half(flow_bar[:, -1, :], 1, source_local)
        first_row = first_base + jnp.where(at_start, inflow, 0.0)
        upstream = jnp.concatenate([first_row[:, None, :], flow_bar[:, :-1, :]], axis=1)
        mass_rows = pack_bar - earlier + flow_bar - upstream
        momentum = friction * flow_bar - (pack_bar - after_seg)
        hour_major = lax.all_to_all(pack_bar, "pipe", split_axis=1, concat_axis=2, tiled=True)
        totals = contract_local(hour_major, contract_map, class_count)
        mass_rows, momentum, totals = (mass_rows, momentum, share_scale * totals)
        mass_next = mass_dual + dual_step * (injection - mass_rows)
        momentum_next = momentum_dual - dual_step * momentum
        contract_next = contract_now + dual_step * (target_now - totals)
        primal_sq = jnp.sum((flow_next - segment_flow) ** 2) + jnp.sum((pack_next - linepack) ** 2)
        dual_sq = (
            jnp.sum((mass_next - mass_dual) ** 2)
            + jnp.sum((momentum_next - momentum_dual) ** 2)
            + jnp.sum((contract_next - contract_now) ** 2)
        )
        primal_total, dual_total = lax.psum((primal_sq, dual_sq), ("pipe", "hour", "seg"))
        weight = jnp.sqrt(weight * jnp.sqrt((dual_total + NORM_EPS) / (primal_total + NORM_EPS)))
        segment_flow, linepack = (flow_next, pack_next)
        mass_dual, momentum_dual, contract_now = (mass_next, momentum_next, contract_next)
    return (
        segment_flow,
        linepack,
        mass_dual,
        momentum_dual,
        contract_now.reshape(contract_dual.shape),
        weight.reshape(1),
    )


def solution(mesh):
    return jax.shard_map(
        on_device,
        mesh=mesh,
        in_specs=(
            P(("groups", "hour"), "seg", "pipe"),
            P(("groups", "hour"), "seg", "pipe"),
            P(("groups", "hour"), "seg", "pipe"),
            P(("groups", "hour"), "seg", "pipe"),
            P(("groups", "hour"), "seg", "pipe", None),
            P(("groups", "hour"), "seg", "pipe"),
            P(("groups", "hour"), "seg", "pipe"),
            P(("groups", "hour"), "seg", "pipe", None),
            P(),
            P("seg", ("groups", "pipe")),
            P("groups"),
            P(("groups", "hour"), None),
        ),
        out_specs=(
            P(("groups", "hour"), "seg", "pipe"),
            P(("groups", "hour"), "seg", "pipe"),
            P(("groups", "hour"), "seg", "pipe"),
            P(("groups", "hour"), "seg", "pipe"),
            P(("groups", "hour"), "seg", "pipe", None),
            P("groups"),
        ),
        check_vma=False,
    )
```

profile of v0, /device:TPU:0, one launch (start us, length us, event | category | flops | bytes accessed | tf_op | source)
XLA Modules:
  0.0 255.9 jit_solution(9958504613072737630)
XLA Ops:
  0.6 2.2 fusion.4
  3.7 3.1 %reshape.116 = f32[4,1,8192]{2,1,0:T(1,128)} reshape(f32[1024,4,8]{2,1,0:T(4,128)S(1)} %bitcast.195) | data formatting | bytes 262144
  6.8 6.3 %all-to-all-start = ((f32[4,1,8192]{2,1,0:T(1,128)}), f32[4,1,8192]{2,1,0:T(1,128)S(1)}, u32[]{:S(2)}, u32[]{:S(2)}) async-start(f32[4,1,8192]{2,1,0:T(1,128)} %reshape.116), calls=%async_computation | async-start | bytes 262144 | tf_op jit(solution)/shard_map/all_to_all | solution.py:141
  14.5 4.5 %collective-permute-start = (f32[2,1,32,256]{3,2,1,0:T(8,128)S(1)}, f32[2,1,32,256]{3,2,1,0:T(8,128)S(1)}, u32[]{:S(2)}, u32[]{:S(2)}) collective-permute-start(f32[2,1,32,256]{3,2,1,0:T(8,128)S(1)} %get-tuple-element.135), channel_id=1, source_target_pairs={{0,2},{1,3},{4,6},{5,7},{8,10},{9,11},{12,14},{13,15},{16,18},{17,... | collective-permute-start | bytes 196616 | tf_op jit(solution)/shard_map/ppermute | solution.py:22
  19.1 14.6 %all_gather.12 = f32[4,8,256]{2,0,1:T(4,128)S(1)} all-gather(f32[4,1,256]{2,0,1:T(4,128)S(1)} %copy.255), channel_id=1, replica_groups=mesh['groups'=2,'pipe'=4,'hour'=2,'seg'=2] {'pipe','seg'}, dimensions={1}, use_global_device_ids=true | all-gather | bytes 36864 | tf_op jit(solution)/shard_map/all_gather | solution.py:36
  33.9 4.3 %scatter_custom_fusion = s32[1024]{0:T(1024)S(1)} fusion(s32[1024]{0:T(1024)S(1)} %compare_select_fusion, s32[1024]{0:T(1024)S(1)} %iota.14, s32[]{:T(128)} %constant.26.clone.1), kind=kCustom, calls=%fused_computation.140 | custom fusion | bytes 4100 | tf_op jit(solution)/shard_map/scatter | solution.py:122
  40.3 2.2 collective-permute-start.3
  47.8 2.5 reshape.117
  50.4 1.8 broadcast_multiply_fusion.1
  52.2 1.9 copy.145
  58.7 4.5 %collective-permute-start.4 = (f32[2,1,32,256]{3,2,1,0:T(8,128)S(1)}, f32[2,1,32,256]{3,2,1,0:T(8,128)S(1)}, u32[]{:S(2)}, u32[]{:S(2)}) collective-permute-start(f32[2,1,32,256]{3,2,1,0:T(8,128)S(1)} %get-tuple-element.131), channel_id=1, source_target_pairs={{0,2},{1,3},{4,6},{5,7},{8,10},{9,11},{12,14},{13,15},{16,18},{17,... | collective-permute-start | bytes 196616 | tf_op jit(solution)/shard_map/ppermute | solution.py:22
  63.3 14.0 %all_gather.13 = f32[4,8,256]{2,0,1:T(4,128)S(1)} all-gather(f32[4,1,256]{2,0,1:T(4,128)S(1)} %slice.182), channel_id=1, replica_groups=mesh['groups'=2,'pipe'=4,'hour'=2,'seg'=2] {'pipe','seg'}, dimensions={1}, use_global_device_ids=true | all-gather | bytes 36864 | tf_op jit(solution)/shard_map/all_gather | solution.py:36
  78.7 2.2 collective-permute-start.6
  84.0 2.0 multiply_reduce_fusion.7
  87.5 4.5 %collective-permute-start.8 = (f32[2,1,32,256]{3,2,1,0:T(8,128)S(1)}, f32[2,1,32,256]{3,2,1,0:T(8,128)S(1)}, u32[]{:S(2)}, u32[]{:S(2)}) collective-permute-start(f32[2,1,32,256]{3,2,1,0:T(8,128)S(1)} %get-tuple-element.127), channel_id=1, source_target_pairs={{0,2},{1,3},{4,6},{5,7},{8,10},{9,11},{12,14},{13,15},{16,18},{17,... | collective-permute-start | bytes 196616 | tf_op jit(solution)/shard_map/ppermute | solution.py:22
  92.0 4.5 %all-to-all-start.1 = ((f32[4,32,256]{2,0,1:T(4,128)}), f32[4,32,256]{2,0,1:T(4,128)S(1)}, u32[]{:S(2)}, u32[]{:S(2)}) async-start(f32[4,32,256]{2,0,1:T(4,128)} %multiply_subtract_fusion.3), calls=%async_computation.1 | async-start | bytes 262144 | tf_op jit(solution)/shard_map/all_to_all | solution.py:159
  98.5 14.6 %all_gather.14 = f32[4,8,256]{2,0,1:T(4,128)S(1)} all-gather(f32[4,1,256]{2,0,1:T(4,128)S(1)} %slice.191), channel_id=1, replica_groups=mesh['groups'=2,'pipe'=4,'hour'=2,'seg'=2] {'pipe','seg'}, dimensions={1}, use_global_device_ids=true | all-gather | bytes 36864 | tf_op jit(solution)/shard_map/all_gather | solution.py:36
  116.3 2.2 collective-permute-start.11
  120.7 2.2 fusion.73
  122.9 1.8 fusion.1
  125.6 3.1 %reshape.118 = f32[4,1,8192]{2,1,0:T(1,128)} reshape(f32[1024,4,8]{2,1,0:T(4,128)S(1)} %bitcast.197) | data formatting | bytes 262144
  128.7 4.5 %all-to-all-start.2 = ((f32[4,1,8192]{2,1,0:T(1,128)}), f32[4,1,8192]{2,1,0:T(1,128)S(1)}, u32[]{:S(2)}, u32[]{:S(2)}) async-start(f32[4,1,8192]{2,1,0:T(1,128)} %reshape.118), calls=%async_computation.2 | async-start | bytes 262144 | tf_op jit(solution)/shard_map/all_to_all | solution.py:141
  135.1 33.5 %all-reduce.1 = (f32[]{:T(128)}, f32[]{:T(128)}) all-reduce(f32[]{:T(128)S(6)} %add.153, f32[]{:T(128)S(6)} %add.155), channel_id=1, replica_groups=mesh['groups'=2,'pipe'=4,'hour'=2,'seg'=2] {'pipe','hour','seg'}, use_global_device_ids=true, to_apply=%region_5.7 | all-reduce | flops 2 | bytes 16 | tf_op jit(solution)/shard_map/psum | solution.py:171
  171.0 2.5 reshape.119
  175.4 1.9 copy.175
  181.3 4.5 %collective-permute-start.12 = (f32[2,1,32,256]{3,2,1,0:T(8,128)S(1)}, f32[2,1,32,256]{3,2,1,0:T(8,128)S(1)}, u32[]{:S(2)}, u32[]{:S(2)}) collective-permute-start(f32[2,1,32,256]{3,2,1,0:T(8,128)S(1)} %get-tuple-element.123), channel_id=1, source_target_pairs={{0,2},{1,3},{4,6},{5,7},{8,10},{9,11},{12,14},{13,15},{16,18},{17,... | collective-permute-start | bytes 196616 | tf_op jit(solution)/shard_map/ppermute | solution.py:22
  187.2 3.5 %all-to-all-start.3 = ((f32[4,32,256]{2,0,1:T(4,128)}), f32[4,32,256]{2,0,1:T(4,128)S(1)}, u32[]{:S(2)}, u32[]{:S(2)}) async-start(f32[4,32,256]{2,0,1:T(4,128)} %multiply_subtract_fusion.1), calls=%async_computation.3 | async-start | bytes 262144 | tf_op jit(solution)/shard_map/all_to_all | solution.py:159
  190.7 14.6 %all_gather.15 = f32[4,8,256]{2,0,1:T(4,128)S(1)} all-gather(f32[4,1,256]{2,0,1:T(4,128)S(1)} %slice.198), channel_id=1, replica_groups=mesh['groups'=2,'pipe'=4,'hour'=2,'seg'=2] {'pipe','seg'}, dimensions={1}, use_global_device_ids=true | all-gather | bytes 36864 | tf_op jit(solution)/shard_map/all_gather | solution.py:36
  209.4 3.0 %collective-permute-start.14 = (f32[2,6,1,256]{1,3,2,0:T(8,128)S(1)}, f32[2,6,1,256]{1,3,2,0:T(8,128)S(1)}, u32[]{:S(2)}, u32[]{:S(2)}) collective-permute-start(f32[2,6,1,256]{1,3,2,0:T(8,128)S(1)} %copy.201), channel_id=1, source_target_pairs={{0,1},{2,3},{4,5},{6,7},{8,9},{10,11},{12,13},{14,15},{16,17},{18,... | collective-permute-start | bytes 36872 | tf_op jit(solution)/shard_map/ppermute | solution.py:22
  213.8 1.8 multiply_reduce_fusion.2
  217.6 2.4 multiply_reduce_fusion.8
  221.4 32.0 %all-reduce = (f32[]{:T(128)}, f32[]{:T(128)}) all-reduce(f32[]{:T(128)S(6)} %add.167, f32[]{:T(128)S(6)} %add.169), channel_id=1, replica_groups=mesh['groups'=2,'pipe'=4,'hour'=2,'seg'=2] {'pipe','hour','seg'}, use_global_device_ids=true, to_apply=%region_12.14 | all-reduce | flops 2 | bytes 16 | tf_op jit(solution)/shard_map/psum | solution.py:171
  (151 shorter events, 40.3 us)
Async XLA Ops:
  2.8 10.3 %copy-start = (f32[4,32,256]{2,1,0:T(8,128)S(1)}, f32[4,32,256]{2,1,0:T(8,128)}, u32[]{:S(2)}) copy-start(f32[4,32,256]{2,1,0:T(8,128)} %param.16) | copy-start | bytes 393220
  2.8 10.3 %copy-start.1 = (f32[4,32,256]{2,1,0:T(8,128)S(1)}, f32[4,32,256]{2,1,0:T(8,128)}, u32[]{:S(2)}) copy-start(f32[4,32,256]{2,1,0:T(8,128)} %param.17) | copy-start | bytes 393220
  3.7 30.2 %copy-start.12 = (s32[1024]{0:T(1024)S(1)}, s32[1024]{0:T(1024)}, u32[]{:S(2)}) copy-start(s32[1024]{0:T(1024)} %param.24) | copy-start | bytes 12292
  3.7 35.3 %copy-start.11 = (s32[32,256]{1,0:T(8,128)S(1)}, s32[32,256]{1,0:T(8,128)}, u32[]{:S(2)}) copy-start(s32[32,256]{1,0:T(8,128)} %param.23) | copy-start | bytes 98308
  3.7 35.3 %copy-start.13 = (f32[16]{0:T(128)S(1)}, f32[16]{0:T(128)}, u32[]{:S(2)}) copy-start(f32[16]{0:T(128)} %param.22) | copy-start | bytes 196
  6.8 39.5 %all-to-all-start = ((f32[4,1,8192]{2,1,0:T(1,128)}), f32[4,1,8192]{2,1,0:T(1,128)S(1)}, u32[]{:S(2)}, u32[]{:S(2)}) async-start(f32[4,1,8192]{2,1,0:T(1,128)} %reshape.116), calls=%async_computation | async-start | bytes 262144 | tf_op jit(solution)/shard_map/all_to_all | solution.py:141
  13.2 26.8 %collective-permute-start.1 = (f32[2,1,32,256]{3,2,1,0:T(8,128)S(1)}, f32[2,1,32,256]{3,2,1,0:T(8,128)S(1)}, u32[]{:S(2)}, u32[]{:S(2)}) collective-permute-start(f32[2,1,32,256]{3,2,1,0:T(8,128)S(1)} %get-tuple-element.136), channel_id=1, source_target_pairs={{2,0},{3,1},{6,4},{7,5},{10,8},{11,9},{14,12},{15,13},{18,16},{19,... | collective-permute-start | bytes 196616 | tf_op jit(solution)/shard_map/ppermute | solution.py:24
  14.5 25.5 %collective-permute-start = (f32[2,1,32,256]{3,2,1,0:T(8,128)S(1)}, f32[2,1,32,256]{3,2,1,0:T(8,128)S(1)}, u32[]{:S(2)}, u32[]{:S(2)}) collective-permute-start(f32[2,1,32,256]{3,2,1,0:T(8,128)S(1)} %get-tuple-element.135), channel_id=1, source_target_pairs={{0,2},{1,3},{4,6},{5,7},{8,10},{9,11},{12,14},{13,15},{16,18},{17,... | collective-permute-start | bytes 196616 | tf_op jit(solution)/shard_map/ppermute | solution.py:22
  40.3 13.8 %collective-permute-start.3 = (f32[2,6,1,256]{3,1,2,0:T(8,128)S(1)}, f32[2,6,1,256]{3,1,2,0:T(8,128)S(1)}, u32[]{:S(2)}, u32[]{:S(2)}) collective-permute-start(f32[2,6,1,256]{3,1,2,0:T(8,128)S(1)} %slice.177), channel_id=1, source_target_pairs={{0,1},{2,3},{4,5},{6,7},{8,9},{10,11},{12,13},{14,15},{16,17},{18,... | collective-permute-start | bytes 36872 | tf_op jit(solution)/shard_map/ppermute | solution.py:22
  42.7 3.4 %collective-permute-start.2 = (f32[2,6,1,256]{1,3,2,0:T(8,128)S(1)}, f32[2,6,1,256]{1,3,2,0:T(8,128)S(1)}, u32[]{:S(2)}, u32[]{:S(2)}) collective-permute-start(f32[2,6,1,256]{1,3,2,0:T(8,128)S(1)} %copy.191), channel_id=1, source_target_pairs={{1,0},{3,2},{5,4},{7,6},{9,8},{11,10},{13,12},{15,14},{17,16},{19,... | collective-permute-start | bytes 36872 | tf_op jit(solution)/shard_map/ppermute | solution.py:24
  52.2 2.0 copy-start.8
  52.2 2.0 copy-start.9
  57.2 26.8 %copy-start.6 = (f32[4,32,256]{2,1,0:T(8,128)S(1)}, f32[4,32,256]{2,1,0:T(8,128)}, u32[]{:S(2)}) copy-start(f32[4,32,256]{2,1,0:T(8,128)} %param.20) | copy-start | bytes 393220
  57.2 21.0 %collective-permute-start.5 = (f32[2,1,32,256]{3,2,1,0:T(8,128)S(1)}, f32[2,1,32,256]{3,2,1,0:T(8,128)S(1)}, u32[]{:S(2)}, u32[]{:S(2)}) collective-permute-start(f32[2,1,32,256]{3,2,1,0:T(8,128)S(1)} %get-tuple-element.132), channel_id=1, source_target_pairs={{2,0},{3,1},{6,4},{7,5},{10,8},{11,9},{14,12},{15,13},{18,16},{19,... | collective-permute-start | bytes 196616 | tf_op jit(solution)/shard_map/ppermute | solution.py:24
  58.7 19.6 %collective-permute-start.4 = (f32[2,1,32,256]{3,2,1,0:T(8,128)S(1)}, f32[2,1,32,256]{3,2,1,0:T(8,128)S(1)}, u32[]{:S(2)}, u32[]{:S(2)}) collective-permute-start(f32[2,1,32,256]{3,2,1,0:T(8,128)S(1)} %get-tuple-element.131), channel_id=1, source_target_pairs={{0,2},{1,3},{4,6},{5,7},{8,10},{9,11},{12,14},{13,15},{16,18},{17,... | collective-permute-start | bytes 196616 | tf_op jit(solution)/shard_map/ppermute | solution.py:22
  78.7 3.7 %collective-permute-start.6 = (f32[2,6,1,256]{1,3,2,0:T(8,128)S(1)}, f32[2,6,1,256]{1,3,2,0:T(8,128)S(1)}, u32[]{:S(2)}, u32[]{:S(2)}) collective-permute-start(f32[2,6,1,256]{1,3,2,0:T(8,128)S(1)} %copy.195), channel_id=1, source_target_pairs={{0,1},{2,3},{4,5},{6,7},{8,9},{10,11},{12,13},{14,15},{16,17},{18,... | collective-permute-start | bytes 36872 | tf_op jit(solution)/shard_map/ppermute | solution.py:22
  81.0 3.1 %collective-permute-start.7 = (f32[2,6,1,256]{3,1,2,0:T(8,128)S(1)}, f32[2,6,1,256]{3,1,2,0:T(8,128)S(1)}, u32[]{:S(2)}, u32[]{:S(2)}) collective-permute-start(f32[2,6,1,256]{3,1,2,0:T(8,128)S(1)} %slice.185), channel_id=1, source_target_pairs={{1,0},{3,2},{5,4},{7,6},{9,8},{11,10},{13,12},{15,14},{17,16},{19,... | collective-permute-start | bytes 36872 | tf_op jit(solution)/shard_map/ppermute | solution.py:24
  86.1 34.6 %copy-start.14 = (f32[4,1,8,128]{3,2,1,0:T(8,128)S(1)}, f32[4,1,8,128]{3,2,1,0:T(8,128)}, u32[]{:S(2)}) copy-start(f32[4,1,8,128]{3,2,1,0:T(8,128)} %param.18) | copy-start | bytes 49156
  86.1 34.6 %copy-start.15 = (s32[4,1024]{1,0:T(4,128)S(1)}, s32[4,1024]{1,0:T(4,128)}, u32[]{:S(2)}) copy-start(s32[4,1024]{1,0:T(4,128)} %param.25) | copy-start | bytes 49156
  86.1 34.6 %copy-start.16 = (f32[4,1,8,128]{3,2,1,0:T(8,128)S(1)}, f32[4,1,8,128]{3,2,1,0:T(8,128)}, u32[]{:S(2)}) copy-start(f32[4,1,8,128]{3,2,1,0:T(8,128)} %param.21) | copy-start | bytes 49156
  86.2 29.8 %collective-permute-start.9 = (f32[2,1,32,256]{3,2,1,0:T(8,128)S(1)}, f32[2,1,32,256]{3,2,1,0:T(8,128)S(1)}, u32[]{:S(2)}, u32[]{:S(2)}) collective-permute-start(f32[2,1,32,256]{3,2,1,0:T(8,128)S(1)} %get-tuple-element.128), channel_id=1, source_target_pairs={{2,0},{3,1},{6,4},{7,5},{10,8},{11,9},{14,12},{15,13},{18,16},{19,... | collective-permute-start | bytes 196616 | tf_op jit(solution)/shard_map/ppermute | solution.py:24
  87.5 28.5 %collective-permute-start.8 = (f32[2,1,32,256]{3,2,1,0:T(8,128)S(1)}, f32[2,1,32,256]{3,2,1,0:T(8,128)S(1)}, u32[]{:S(2)}, u32[]{:S(2)}) collective-permute-start(f32[2,1,32,256]{3,2,1,0:T(8,128)S(1)} %get-tuple-element.127), channel_id=1, source_target_pairs={{0,2},{1,3},{4,6},{5,7},{8,10},{9,11},{12,14},{13,15},{16,18},{17,... | collective-permute-start | bytes 196616 | tf_op jit(solution)/shard_map/ppermute | solution.py:22
  92.0 28.6 %all-to-all-start.1 = ((f32[4,32,256]{2,0,1:T(4,128)}), f32[4,32,256]{2,0,1:T(4,128)S(1)}, u32[]{:S(2)}, u32[]{:S(2)}) async-start(f32[4,32,256]{2,0,1:T(4,128)} %multiply_subtract_fusion.3), calls=%async_computation.1 | async-start | bytes 262144 | tf_op jit(solution)/shard_map/all_to_all | solution.py:159
  116.3 61.0 %collective-permute-start.11 = (f32[2,6,1,256]{3,1,2,0:T(8,128)S(1)}, f32[2,6,1,256]{3,1,2,0:T(8,128)S(1)}, u32[]{:S(2)}, u32[]{:S(2)}) collective-permute-start(f32[2,6,1,256]{3,1,2,0:T(8,128)S(1)} %slice.193), channel_id=1, source_target_pairs={{0,1},{2,3},{4,5},{6,7},{8,9},{10,11},{12,13},{14,15},{16,17},{18,... | collective-permute-start | bytes 36872 | tf_op jit(solution)/shard_map/ppermute | solution.py:22
  119.3 13.9 %collective-permute-start.10 = (f32[2,6,1,256]{1,3,2,0:T(8,128)}, f32[2,6,1,256]{1,3,2,0:T(8,128)}, u32[]{:S(2)}, u32[]{:S(2)}) collective-permute-start(f32[2,6,1,256]{1,3,2,0:T(8,128)} %copy.197), channel_id=1, source_target_pairs={{1,0},{3,2},{5,4},{7,6},{9,8},{11,10},{13,12},{15,14},{17,16},{19,... | collective-permute-start | bytes 36872 | tf_op jit(solution)/shard_map/ppermute | solution.py:24
  128.7 41.3 %all-to-all-start.2 = ((f32[4,1,8192]{2,1,0:T(1,128)}), f32[4,1,8192]{2,1,0:T(1,128)S(1)}, u32[]{:S(2)}, u32[]{:S(2)}) async-start(f32[4,1,8192]{2,1,0:T(1,128)} %reshape.118), calls=%async_computation.2 | async-start | bytes 262144 | tf_op jit(solution)/shard_map/all_to_all | solution.py:141
  180.0 27.6 %collective-permute-start.13 = (f32[2,1,32,256]{3,2,1,0:T(8,128)S(1)}, f32[2,1,32,256]{3,2,1,0:T(8,128)S(1)}, u32[]{:S(2)}, u32[]{:S(2)}) collective-permute-start(f32[2,1,32,256]{3,2,1,0:T(8,128)S(1)} %get-tuple-element.124), channel_id=1, source_target_pairs={{2,0},{3,1},{6,4},{7,5},{10,8},{11,9},{14,12},{15,13},{18,16},{19,... | collective-permute-start | bytes 196616 | tf_op jit(solution)/shard_map/ppermute | solution.py:24
  181.3 26.3 %collective-permute-start.12 = (f32[2,1,32,256]{3,2,1,0:T(8,128)S(1)}, f32[2,1,32,256]{3,2,1,0:T(8,128)S(1)}, u32[]{:S(2)}, u32[]{:S(2)}) collective-permute-start(f32[2,1,32,256]{3,2,1,0:T(8,128)S(1)} %get-tuple-element.123), channel_id=1, source_target_pairs={{0,2},{1,3},{4,6},{5,7},{8,10},{9,11},{12,14},{13,15},{16,18},{17,... | collective-permute-start | bytes 196616 | tf_op jit(solution)/shard_map/ppermute | solution.py:22
  187.2 26.6 %copy-start.7 = (f32[4,32,256]{2,1,0:T(8,128)S(1)}, f32[4,32,256]{2,1,0:T(8,128)}, u32[]{:S(2)}) copy-start(f32[4,32,256]{2,1,0:T(8,128)} %param.20) | copy-start | bytes 393220
  187.2 30.4 %all-to-all-start.3 = ((f32[4,32,256]{2,0,1:T(4,128)}), f32[4,32,256]{2,0,1:T(4,128)S(1)}, u32[]{:S(2)}, u32[]{:S(2)}) async-start(f32[4,32,256]{2,0,1:T(4,128)} %multiply_subtract_fusion.1), calls=%async_computation.3 | async-start | bytes 262144 | tf_op jit(solution)/shard_map/all_to_all | solution.py:159
  207.9 5.8 %collective-permute-start.15 = (f32[2,6,1,256]{3,1,2,0:T(8,128)S(1)}, f32[2,6,1,256]{3,1,2,0:T(8,128)S(1)}, u32[]{:S(2)}, u32[]{:S(2)}) collective-permute-start(f32[2,6,1,256]{3,1,2,0:T(8,128)S(1)} %slice.201), channel_id=1, source_target_pairs={{1,0},{3,2},{5,4},{7,6},{9,8},{11,10},{13,12},{15,14},{17,16},{19,... | collective-permute-start | bytes 36872 | tf_op jit(solution)/shard_map/ppermute | solution.py:24
  209.4 4.2 %collective-permute-start.14 = (f32[2,6,1,256]{1,3,2,0:T(8,128)S(1)}, f32[2,6,1,256]{1,3,2,0:T(8,128)S(1)}, u32[]{:S(2)}, u32[]{:S(2)}) collective-permute-start(f32[2,6,1,256]{1,3,2,0:T(8,128)S(1)} %copy.201), channel_id=1, source_target_pairs={{0,1},{2,3},{4,5},{6,7},{8,9},{10,11},{12,13},{14,15},{16,17},{18,... | collective-permute-start | bytes 36872 | tf_op jit(solution)/shard_map/ppermute | solution.py:22
  (5 other events, 9.7 us)
where the time goes:
time: 257 us; the launch traced here: 256 us
  blocking collectives  123 us (48%)
  starting transfers between devices  57.3 us (22%)
  local copies, waits for them, and re-layouts  34.9 us (14%)
  other arithmetic  15.8 us (6%)
  between operations  12.1 us (5%)
  matrix products  8.66 us (3%)
  waiting for transfers between devices  3.97 us (2%)
    psum x2, blocking collectives, on_device(): lax.psum((primal_sq, dual_sq), ('pipe', 'hour', 'seg'))  65.5 us
    all_gather x4, blocking collectives, other_half(): lax.all_gather(edge_row[:, None, :], ('pipe', 'seg'), axis=1, tiled=True)  57.8 us
    ppermute x8, starting transfers between devices, padded(): lax.ppermute(tail, axis, [(i, (i + 1) % count) for i in range(ends)])  27.9 us
    unnamed x55, local copies, waits for them, and re-layouts  17 us
    all_to_all x2, starting transfers between devices, on_device(): lax.all_to_all(hour_spread, 'pipe', split_axis=2, concat_axis=1, tiled=True)  10.8 us
    ppermute x8, starting transfers between devices, padded(): lax.ppermute(head, axis, [((i + 1) % count, i) for i in range(ends)])  10.6 us
    all_to_all x2, starting transfers between devices, on_device(): lax.all_to_all(pack_bar, 'pipe', split_axis=1, concat_axis=2, tiled=True)  7.96 us
  transfers between devices with their start and end apart: 20, of which 3 were waited for; matrix products, arithmetic and copies ran while one was open for 16% of the time, Pallas kernels for 0%

commit v1 on v0

--- a/solution.py
+++ b/solution.py
@@ -9,6 +9,19 @@
 PACK_CAP = 2.5
 STEP_SCALE = 0.25
 NORM_EPS = 1e-06
+
+
+def ring_gather(x, axis, dim):
+    length, here, rows = (lax.axis_size(axis), lax.axis_index(axis), x.shape[dim])
+    right = [(i, (i + 1) % length) for i in range(length)]
+    out = jnp.zeros((*x.shape[:dim], length * rows, *x.shape[dim + 1 :]), x.dtype)
+    held = x
+    for step in range(length):
+        owner = (here - step) % length
+        out = lax.dynamic_update_slice_in_dim(out, held, owner * rows, axis=dim)
+        if step < length - 1:
+            held = lax.ppermute(held, axis, right)
+    return out
 
 
 def padded(cells, sides, width):
@@ -33,7 +46,7 @@
 
 
 def other_half(edge_row, half_index, partner_local):
-    gathered = lax.all_gather(edge_row[:, None, :], ("pipe", "seg"), axis=1, tiled=True)
+    gathered = ring_gather(edge_row[:, None, :], ("pipe", "seg"), 1)
     hour_rows, row_count, row_width = gathered.shape
     seg_count = lax.axis_size("seg")
     picked = gathered.reshape(hour_rows, row_count // seg_count, seg_count, row_width)[

time: 257 us -> 313 us (1.22)
  waiting for transfers between devices: 3.97 us -> 116 us
  blocking collectives: 123 us -> 64.1 us
    ppermute x0 -> x28, waiting for transfers between devices: none -> 112 us  [ring_gather(): held = lax.ppermute(held, axis, right)]
    all_gather x4 -> x0, blocking collectives: 57.8 us -> none  [other_half(): lax.all_gather(edge_row[:, None, :], ('pipe', 'seg'), axis=1, tiled=True)]
    ppermute x0 -> x28, starting transfers between devices: none -> 5.19 us  [ring_gather(): held = lax.ppermute(held, axis, right)]
    unnamed x55 -> x48, local copies, waits for them, and re-layouts: 17 us -> 17 us
  transfers between devices with their start and end apart: 20 -> 48, of which waited for: 3 -> 27; matrix products, arithmetic and copies ran while one was open for 16% -> 15% of each run, Pallas kernels for 0% -> 0%
where the time goes in v1:
time: 313 us; the launch traced here: 312 us
  waiting for transfers between devices  116 us (37%)
  blocking collectives  64.1 us (20%)
  starting transfers between devices  57.2 us (18%)
  local copies, waits for them, and re-layouts  36.9 us (12%)
  other arithmetic  16.4 us (5%)
  between operations  12.2 us (4%)
  matrix products  8.93 us (3%)
    ppermute x28, waiting for transfers between devices, ring_gather(): held = lax.ppermute(held, axis, right)  112 us
    psum x2, blocking collectives, on_device(): lax.psum((primal_sq, dual_sq), ('pipe', 'hour', 'seg'))  64.1 us
    ppermute x8, starting transfers between devices, padded(): lax.ppermute(tail, axis, [(i, (i + 1) % count) for i in range(ends)])  25.3 us
    unnamed x48, local copies, waits for them, and re-layouts  17 us
    ppermute x8, starting transfers between devices, padded(): lax.ppermute(head, axis, [((i + 1) % count, i) for i in range(ends)])  10.4 us
    all_to_all x2, starting transfers between devices, on_device(): lax.all_to_all(hour_spread, 'pipe', split_axis=2, concat_axis=1, tiled=True)  9.64 us
    all_to_all x2, starting transfers between devices, on_device(): lax.all_to_all(pack_bar, 'pipe', split_axis=1, concat_axis=2, tiled=True)  6.66 us
  transfers between devices with their start and end apart: 48, of which 27 were waited for; matrix products, arithmetic and copies ran while one was open for 15% of the time, Pallas kernels for 0%

profile of v1, /device:TPU:0, one launch (start us, length us, event | category | flops | bytes accessed | tf_op | source)
XLA Modules:
  0.0 311.7 jit_solution(13467952064483631409)
XLA Ops:
  6.8 6.3 %all-to-all-start = ((f32[4,1,8192]{2,1,0:T(1,128)}), f32[4,1,8192]{2,1,0:T(1,128)S(1)}, u32[]{:S(2)}, u32[]{:S(2)}) async-start(f32[4,1,8192]{2,1,0:T(1,128)} %reshape.116), calls=%async_computation | async-start | bytes 262144 | tf_op jit(solution)/shard_map/all_to_all | solution.py:154
  14.5 4.5 %collective-permute-start = (f32[2,1,32,256]{3,2,1,0:T(8,128)S(1)}, f32[2,1,32,256]{3,2,1,0:T(8,128)S(1)}, u32[]{:S(2)}, u32[]{:S(2)}) collective-permute-start(f32[2,1,32,256]{3,2,1,0:T(8,128)S(1)} %get-tuple-element.141), channel_id=1, source_target_pairs={{0,2},{1,3},{4,6},{5,7},{8,10},{9,11},{12,14},{13,15},{16,18},{17,... | collective-permute-start | bytes 196616 | tf_op jit(solution)/shard_map/ppermute | solution.py:35
  19.3 4.3 %scatter_custom_fusion = s32[1024]{0:T(1024)S(1)} fusion(s32[1024]{0:T(1024)S(1)} %compare_select_fusion, s32[1024]{0:T(1024)S(1)} %iota.14, s32[]{:T(128)} %constant.168.clone.1), kind=kCustom, calls=%fused_computation.172 | custom fusion | bytes 4100 | tf_op jit(solution)/shard_map/scatter | solution.py:135
  29.6 4.8 %collective-permute-done.5 = f32[4,1,256]{2,1,0:T(1,128)S(1)} collective-permute-done((f32[4,1,256]{2,1,0:T(1,128)S(1)}, f32[4,1,256]{2,1,0:T(1,128)S(1)}, u32[]{:S(2)}, u32[]{:S(2)}) %collective-permute-start.5) | collective-permute-done | bytes 4128 | tf_op jit(solution)/shard_map/ppermute | solution.py:23
  34.4 4.8 %collective-permute-done.6 = f32[4,1,256]{2,1,0:T(1,128)S(1)} collective-permute-done((f32[4,1,256]{2,1,0:T(1,128)S(1)}, f32[4,1,256]{2,1,0:T(1,128)S(1)}, u32[]{:S(2)}, u32[]{:S(2)}) %collective-permute-start.6) | collective-permute-done | bytes 4128 | tf_op jit(solution)/shard_map/ppermute | solution.py:23
  39.2 4.8 %collective-permute-done.7 = f32[4,1,256]{2,1,0:T(1,128)S(1)} collective-permute-done((f32[4,1,256]{2,1,0:T(1,128)S(1)}, f32[4,1,256]{2,1,0:T(1,128)S(1)}, u32[]{:S(2)}, u32[]{:S(2)}) %collective-permute-start.7) | collective-permute-done | bytes 4128 | tf_op jit(solution)/shard_map/ppermute | solution.py:23
  44.1 4.8 %collective-permute-done.8 = f32[4,1,256]{2,1,0:T(1,128)S(1)} collective-permute-done((f32[4,1,256]{2,1,0:T(1,128)S(1)}, f32[4,1,256]{2,1,0:T(1,128)S(1)}, u32[]{:S(2)}, u32[]{:S(2)}) %collective-permute-start.8) | collective-permute-done | bytes 4128 | tf_op jit(solution)/shard_map/ppermute | solution.py:23
  48.9 4.8 %collective-permute-done.9 = f32[4,1,256]{2,1,0:T(1,128)S(1)} collective-permute-done((f32[4,1,256]{2,1,0:T(1,128)S(1)}, f32[4,1,256]{2,1,0:T(1,128)S(1)}, u32[]{:S(2)}, u32[]{:S(2)}) %collective-permute-start.9) | collective-permute-done | bytes 4128 | tf_op jit(solution)/shard_map/ppermute | solution.py:23
  76.0 4.5 %collective-permute-start.11 = (f32[2,1,32,256]{3,2,1,0:T(8,128)S(1)}, f32[2,1,32,256]{3,2,1,0:T(8,128)S(1)}, u32[]{:S(2)}, u32[]{:S(2)}) collective-permute-start(f32[2,1,32,256]{3,2,1,0:T(8,128)S(1)} %get-tuple-element.137), channel_id=1, source_target_pairs={{0,2},{1,3},{4,6},{5,7},{8,10},{9,11},{12,14},{13,15},{16,18},{17,... | collective-permute-start | bytes 196616 | tf_op jit(solution)/shard_map/ppermute | solution.py:35
  83.4 3.4 %collective-permute-done.15 = f32[4,1,256]{2,0,1:T(4,128)S(1)} collective-permute-done((f32[4,1,256]{2,0,1:T(4,128)S(1)}, f32[4,1,256]{2,0,1:T(4,128)S(1)}, u32[]{:S(2)}, u32[]{:S(2)}) %collective-permute-start.15) | collective-permute-done | bytes 4128 | tf_op jit(solution)/shard_map/ppermute | solution.py:23
  86.8 4.8 %collective-permute-done.16 = f32[4,1,256]{2,0,1:T(4,128)S(1)} collective-permute-done((f32[4,1,256]{2,0,1:T(4,128)S(1)}, f32[4,1,256]{2,0,1:T(4,128)S(1)}, u32[]{:S(2)}, u32[]{:S(2)}) %collective-permute-start.16) | collective-permute-done | bytes 4128 | tf_op jit(solution)/shard_map/ppermute | solution.py:23
  91.6 4.8 %collective-permute-done.17 = f32[4,1,256]{2,0,1:T(4,128)S(1)} collective-permute-done((f32[4,1,256]{2,0,1:T(4,128)S(1)}, f32[4,1,256]{2,0,1:T(4,128)S(1)}, u32[]{:S(2)}, u32[]{:S(2)}) %collective-permute-start.17) | collective-permute-done | bytes 4128 | tf_op jit(solution)/shard_map/ppermute | solution.py:23
  96.5 4.8 %collective-permute-done.18 = f32[4,1,256]{2,0,1:T(4,128)S(1)} collective-permute-done((f32[4,1,256]{2,0,1:T(4,128)S(1)}, f32[4,1,256]{2,0,1:T(4,128)S(1)}, u32[]{:S(2)}, u32[]{:S(2)}) %collective-permute-start.18) | collective-permute-done | bytes 4128 | tf_op jit(solution)/shard_map/ppermute | solution.py:23
  101.3 4.8 %collective-permute-done.19 = f32[4,1,256]{2,0,1:T(4,128)S(1)} collective-permute-done((f32[4,1,256]{2,0,1:T(4,128)S(1)}, f32[4,1,256]{2,0,1:T(4,128)S(1)}, u32[]{:S(2)}, u32[]{:S(2)}) %collective-permute-start.19) | collective-permute-done | bytes 4128 | tf_op jit(solution)/shard_map/ppermute | solution.py:23
  106.1 4.8 %collective-permute-done.20 = f32[4,1,256]{2,0,1:T(4,128)S(1)} collective-permute-done((f32[4,1,256]{2,0,1:T(4,128)S(1)}, f32[4,1,256]{2,0,1:T(4,128)S(1)}, u32[]{:S(2)}, u32[]{:S(2)}) %collective-permute-start.20) | collective-permute-done | bytes 4128 | tf_op jit(solution)/shard_map/ppermute | solution.py:23
  121.2 4.5 %collective-permute-start.22 = (f32[2,1,32,256]{3,2,1,0:T(8,128)S(1)}, f32[2,1,32,256]{3,2,1,0:T(8,128)S(1)}, u32[]{:S(2)}, u32[]{:S(2)}) collective-permute-start(f32[2,1,32,256]{3,2,1,0:T(8,128)S(1)} %get-tuple-element.133), channel_id=1, source_target_pairs={{0,2},{1,3},{4,6},{5,7},{8,10},{9,11},{12,14},{13,15},{16,18},{17,... | collective-permute-start | bytes 196616 | tf_op jit(solution)/shard_map/ppermute | solution.py:35
  127.2 4.8 %collective-permute-done.26 = f32[4,1,256]{2,0,1:T(4,128)S(1)} collective-permute-done((f32[4,1,256]{2,0,1:T(4,128)S(1)}, f32[4,1,256]{2,0,1:T(4,128)S(1)}, u32[]{:S(2)}, u32[]{:S(2)}) %collective-permute-start.26) | collective-permute-done | bytes 4128 | tf_op jit(solution)/shard_map/ppermute | solution.py:23
  132.0 4.8 %collective-permute-done.27 = f32[4,1,256]{2,0,1:T(4,128)S(1)} collective-permute-done((f32[4,1,256]{2,0,1:T(4,128)S(1)}, f32[4,1,256]{2,0,1:T(4,128)S(1)}, u32[]{:S(2)}, u32[]{:S(2)}) %collective-permute-start.27) | collective-permute-done | bytes 4128 | tf_op jit(solution)/shard_map/ppermute | solution.py:23
  136.8 4.8 %collective-permute-done.28 = f32[4,1,256]{2,0,1:T(4,128)S(1)} collective-permute-done((f32[4,1,256]{2,0,1:T(4,128)S(1)}, f32[4,1,256]{2,0,1:T(4,128)S(1)}, u32[]{:S(2)}, u32[]{:S(2)}) %collective-permute-start.28) | collective-permute-done | bytes 4128 | tf_op jit(solution)/shard_map/ppermute | solution.py:23
  141.6 4.8 %collective-permute-done.29 = f32[4,1,256]{2,0,1:T(4,128)S(1)} collective-permute-done((f32[4,1,256]{2,0,1:T(4,128)S(1)}, f32[4,1,256]{2,0,1:T(4,128)S(1)}, u32[]{:S(2)}, u32[]{:S(2)}) %collective-permute-start.29) | collective-permute-done | bytes 4128 | tf_op jit(solution)/shard_map/ppermute | solution.py:23
  146.5 4.8 %collective-permute-done.30 = f32[4,1,256]{2,0,1:T(4,128)S(1)} collective-permute-done((f32[4,1,256]{2,0,1:T(4,128)S(1)}, f32[4,1,256]{2,0,1:T(4,128)S(1)}, u32[]{:S(2)}, u32[]{:S(2)}) %collective-permute-start.30) | collective-permute-done | bytes 4128 | tf_op jit(solution)/shard_map/ppermute | solution.py:23
  151.3 4.8 %collective-permute-done.31 = f32[4,1,256]{2,0,1:T(4,128)S(1)} collective-permute-done((f32[4,1,256]{2,0,1:T(4,128)S(1)}, f32[4,1,256]{2,0,1:T(4,128)S(1)}, u32[]{:S(2)}, u32[]{:S(2)}) %collective-permute-start.31) | collective-permute-done | bytes 4128 | tf_op jit(solution)/shard_map/ppermute | solution.py:23
  175.8 33.7 %all-reduce.1 = (f32[]{:T(128)}, f32[]{:T(128)}) all-reduce(f32[]{:T(128)S(6)} %add.280, f32[]{:T(128)S(6)} %add.282), channel_id=1, replica_groups=mesh['groups'=2,'pipe'=4,'hour'=2,'seg'=2] {'pipe','hour','seg'}, use_global_device_ids=true, to_apply=%region_5.7 | all-reduce | flops 2 | bytes 16 | tf_op jit(solution)/shard_map/psum | solution.py:184
  212.6 3.4 %reshape.119 = f32[1024,4,8]{2,1,0:T(4,128)S(1)} reshape(f32[4,8192]{1,0:T(4,128)} %reduce.1) | data formatting | bytes 262144
  228.6 4.5 %collective-permute-start.33 = (f32[2,1,32,256]{3,2,1,0:T(8,128)S(1)}, f32[2,1,32,256]{3,2,1,0:T(8,128)S(1)}, u32[]{:S(2)}, u32[]{:S(2)}) collective-permute-start(f32[2,1,32,256]{3,2,1,0:T(8,128)S(1)} %get-tuple-element.129), channel_id=1, source_target_pairs={{0,2},{1,3},{4,6},{5,7},{8,10},{9,11},{12,14},{13,15},{16,18},{17,... | collective-permute-start | bytes 196616 | tf_op jit(solution)/shard_map/ppermute | solution.py:35
  235.6 4.4 %collective-permute-done.37 = f32[4,1,256]{2,0,1:T(4,128)S(1)} collective-permute-done((f32[4,1,256]{2,0,1:T(4,128)S(1)}, f32[4,1,256]{2,0,1:T(4,128)S(1)}, u32[]{:S(2)}, u32[]{:S(2)}) %collective-permute-start.37) | collective-permute-done | bytes 4128 | tf_op jit(solution)/shard_map/ppermute | solution.py:23
  240.0 4.8 %collective-permute-done.38 = f32[4,1,256]{2,0,1:T(4,128)S(1)} collective-permute-done((f32[4,1,256]{2,0,1:T(4,128)S(1)}, f32[4,1,256]{2,0,1:T(4,128)S(1)}, u32[]{:S(2)}, u32[]{:S(2)}) %collective-permute-start.38) | collective-permute-done | bytes 4128 | tf_op jit(solution)/shard_map/ppermute | solution.py:23
  244.8 4.8 %collective-permute-done.39 = f32[4,1,256]{2,0,1:T(4,128)S(1)} collective-permute-done((f32[4,1,256]{2,0,1:T(4,128)S(1)}, f32[4,1,256]{2,0,1:T(4,128)S(1)}, u32[]{:S(2)}, u32[]{:S(2)}) %collective-permute-start.39) | collective-permute-done | bytes 4128 | tf_op jit(solution)/shard_map/ppermute | solution.py:23
  249.7 4.8 %collective-permute-done.40 = f32[4,1,256]{2,0,1:T(4,128)S(1)} collective-permute-done((f32[4,1,256]{2,0,1:T(4,128)S(1)}, f32[4,1,256]{2,0,1:T(4,128)S(1)}, u32[]{:S(2)}, u32[]{:S(2)}) %collective-permute-start.40) | collective-permute-done | bytes 4128 | tf_op jit(solution)/shard_map/ppermute | solution.py:23
  254.5 4.8 %collective-permute-done.41 = f32[4,1,256]{2,0,1:T(4,128)S(1)} collective-permute-done((f32[4,1,256]{2,0,1:T(4,128)S(1)}, f32[4,1,256]{2,0,1:T(4,128)S(1)}, u32[]{:S(2)}, u32[]{:S(2)}) %collective-permute-start.41) | collective-permute-done | bytes 4128 | tf_op jit(solution)/shard_map/ppermute | solution.py:23
  259.3 4.8 %collective-permute-done.42 = f32[4,1,256]{2,0,1:T(4,128)S(1)} collective-permute-done((f32[4,1,256]{2,0,1:T(4,128)S(1)}, f32[4,1,256]{2,0,1:T(4,128)S(1)}, u32[]{:S(2)}, u32[]{:S(2)}) %collective-permute-start.42) | collective-permute-done | bytes 4128 | tf_op jit(solution)/shard_map/ppermute | solution.py:23
  278.9 30.3 %all-reduce = (f32[]{:T(128)}, f32[]{:T(128)}) all-reduce(f32[]{:T(128)S(6)} %add.294, f32[]{:T(128)S(6)} %add.296), channel_id=1, replica_groups=mesh['groups'=2,'pipe'=4,'hour'=2,'seg'=2] {'pipe','hour','seg'}, use_global_device_ids=true, to_apply=%region_12.14 | all-reduce | flops 2 | bytes 16 | tf_op jit(solution)/shard_map/psum | solution.py:184
  (233 shorter events, 94.2 us)
Async XLA Ops:
  6.8 53.3 %all-to-all-start = ((f32[4,1,8192]{2,1,0:T(1,128)}), f32[4,1,8192]{2,1,0:T(1,128)S(1)}, u32[]{:S(2)}, u32[]{:S(2)}) async-start(f32[4,1,8192]{2,1,0:T(1,128)} %reshape.116), calls=%async_computation | async-start | bytes 262144 | tf_op jit(solution)/shard_map/all_to_all | solution.py:154
  13.2 41.5 %collective-permute-start.1 = (f32[2,1,32,256]{3,2,1,0:T(8,128)S(1)}, f32[2,1,32,256]{3,2,1,0:T(8,128)S(1)}, u32[]{:S(2)}, u32[]{:S(2)}) collective-permute-start(f32[2,1,32,256]{3,2,1,0:T(8,128)S(1)} %get-tuple-element.142), channel_id=1, source_target_pairs={{2,0},{3,1},{6,4},{7,5},{10,8},{11,9},{14,12},{15,13},{18,16},{19,... | collective-permute-start | bytes 196616 | tf_op jit(solution)/shard_map/ppermute | solution.py:37
  14.5 40.2 %collective-permute-start = (f32[2,1,32,256]{3,2,1,0:T(8,128)S(1)}, f32[2,1,32,256]{3,2,1,0:T(8,128)S(1)}, u32[]{:S(2)}, u32[]{:S(2)}) collective-permute-start(f32[2,1,32,256]{3,2,1,0:T(8,128)S(1)} %get-tuple-element.141), channel_id=1, source_target_pairs={{0,2},{1,3},{4,6},{5,7},{8,10},{9,11},{12,14},{13,15},{16,18},{17,... | collective-permute-start | bytes 196616 | tf_op jit(solution)/shard_map/ppermute | solution.py:35
  19.0 5.7 %collective-permute-start.3 = (f32[4,1,256]{2,1,0:T(1,128)S(1)}, f32[4,1,256]{2,1,0:T(1,128)S(1)}, u32[]{:S(2)}, u32[]{:S(2)}) collective-permute-start(f32[4,1,256]{2,1,0:T(1,128)S(1)} %slice.129), channel_id=1, source_target_pairs={{0,1},{1,4},{4,5},{5,8},{8,9},{9,12},{12,13},{13,0},{2,3},{3,6},{6... | collective-permute-start | bytes 12296 | tf_op jit(solution)/shard_map/ppermute | solution.py:23
  24.7 4.8 %collective-permute-start.4 = (f32[4,1,256]{2,1,0:T(1,128)S(1)}, f32[4,1,256]{2,1,0:T(1,128)S(1)}, u32[]{:S(2)}, u32[]{:S(2)}) collective-permute-start(f32[4,1,256]{2,1,0:T(1,128)S(1)} %collective-permute-done.3), channel_id=1, source_target_pairs={{0,1},{1,4},{4,5},{5,8},{8,9},{9,12},{12,13},{13,0},{2,3},{3,6},{6... | collective-permute-start | bytes 12296 | tf_op jit(solution)/shard_map/ppermute | solution.py:23
  29.6 4.8 %collective-permute-start.5 = (f32[4,1,256]{2,1,0:T(1,128)S(1)}, f32[4,1,256]{2,1,0:T(1,128)S(1)}, u32[]{:S(2)}, u32[]{:S(2)}) collective-permute-start(f32[4,1,256]{2,1,0:T(1,128)S(1)} %collective-permute-done.4), channel_id=1, source_target_pairs={{0,1},{1,4},{4,5},{5,8},{8,9},{9,12},{12,13},{13,0},{2,3},{3,6},{6... | collective-permute-start | bytes 12296 | tf_op jit(solution)/shard_map/ppermute | solution.py:23
  34.4 4.8 %collective-permute-start.6 = (f32[4,1,256]{2,1,0:T(1,128)S(1)}, f32[4,1,256]{2,1,0:T(1,128)S(1)}, u32[]{:S(2)}, u32[]{:S(2)}) collective-permute-start(f32[4,1,256]{2,1,0:T(1,128)S(1)} %collective-permute-done.5), channel_id=1, source_target_pairs={{0,1},{1,4},{4,5},{5,8},{8,9},{9,12},{12,13},{13,0},{2,3},{3,6},{6... | collective-permute-start | bytes 12296 | tf_op jit(solution)/shard_map/ppermute | solution.py:23
  39.2 4.8 %collective-permute-start.7 = (f32[4,1,256]{2,1,0:T(1,128)S(1)}, f32[4,1,256]{2,1,0:T(1,128)S(1)}, u32[]{:S(2)}, u32[]{:S(2)}) collective-permute-start(f32[4,1,256]{2,1,0:T(1,128)S(1)} %collective-permute-done.6), channel_id=1, source_target_pairs={{0,1},{1,4},{4,5},{5,8},{8,9},{9,12},{12,13},{13,0},{2,3},{3,6},{6... | collective-permute-start | bytes 12296 | tf_op jit(solution)/shard_map/ppermute | solution.py:23
  44.0 4.8 %collective-permute-start.8 = (f32[4,1,256]{2,1,0:T(1,128)S(1)}, f32[4,1,256]{2,1,0:T(1,128)S(1)}, u32[]{:S(2)}, u32[]{:S(2)}) collective-permute-start(f32[4,1,256]{2,1,0:T(1,128)S(1)} %collective-permute-done.7), channel_id=1, source_target_pairs={{0,1},{1,4},{4,5},{5,8},{8,9},{9,12},{12,13},{13,0},{2,3},{3,6},{6... | collective-permute-start | bytes 12296 | tf_op jit(solution)/shard_map/ppermute | solution.py:23
  55.0 12.9 %collective-permute-start.10 = (f32[2,6,1,256]{3,1,2,0:T(8,128)S(1)}, f32[2,6,1,256]{3,1,2,0:T(8,128)S(1)}, u32[]{:S(2)}, u32[]{:S(2)}) collective-permute-start(f32[2,6,1,256]{3,1,2,0:T(8,128)S(1)} %slice.176), channel_id=1, source_target_pairs={{0,1},{2,3},{4,5},{6,7},{8,9},{10,11},{12,13},{14,15},{16,17},{18,... | collective-permute-start | bytes 36872 | tf_op jit(solution)/shard_map/ppermute | solution.py:35
  69.9 91.5 %all-to-all-start.1 = ((f32[4,32,256]{2,0,1:T(4,128)}), f32[4,32,256]{2,0,1:T(4,128)S(1)}, u32[]{:S(2)}, u32[]{:S(2)}) async-start(f32[4,32,256]{2,0,1:T(4,128)} %multiply_subtract_fusion.3), calls=%async_computation.1 | async-start | bytes 262144 | tf_op jit(solution)/shard_map/all_to_all | solution.py:172
  73.5 8.5 %collective-permute-start.14 = (f32[4,1,256]{2,0,1:T(4,128)S(1)}, f32[4,1,256]{2,0,1:T(4,128)S(1)}, u32[]{:S(2)}, u32[]{:S(2)}) collective-permute-start(f32[4,1,256]{2,0,1:T(4,128)S(1)} %get-tuple-element.147), channel_id=1, source_target_pairs={{0,1},{1,4},{4,5},{5,8},{8,9},{9,12},{12,13},{13,0},{2,3},{3,6},{6... | collective-permute-start | bytes 12296 | tf_op jit(solution)/shard_map/ppermute | solution.py:23
  74.6 37.3 %collective-permute-start.12 = (f32[2,1,32,256]{3,2,1,0:T(8,128)S(1)}, f32[2,1,32,256]{3,2,1,0:T(8,128)S(1)}, u32[]{:S(2)}, u32[]{:S(2)}) collective-permute-start(f32[2,1,32,256]{3,2,1,0:T(8,128)S(1)} %get-tuple-element.138), channel_id=1, source_target_pairs={{2,0},{3,1},{6,4},{7,5},{10,8},{11,9},{14,12},{15,13},{18,16},{19,... | collective-permute-start | bytes 196616 | tf_op jit(solution)/shard_map/ppermute | solution.py:37
  76.0 35.9 %collective-permute-start.11 = (f32[2,1,32,256]{3,2,1,0:T(8,128)S(1)}, f32[2,1,32,256]{3,2,1,0:T(8,128)S(1)}, u32[]{:S(2)}, u32[]{:S(2)}) collective-permute-start(f32[2,1,32,256]{3,2,1,0:T(8,128)S(1)} %get-tuple-element.137), channel_id=1, source_target_pairs={{0,2},{1,3},{4,6},{5,7},{8,10},{9,11},{12,14},{13,15},{16,18},{17,... | collective-permute-start | bytes 196616 | tf_op jit(solution)/shard_map/ppermute | solution.py:35
  81.9 4.9 %collective-permute-start.15 = (f32[4,1,256]{2,0,1:T(4,128)S(1)}, f32[4,1,256]{2,0,1:T(4,128)S(1)}, u32[]{:S(2)}, u32[]{:S(2)}) collective-permute-start(f32[4,1,256]{2,0,1:T(4,128)S(1)} %collective-permute-done.14), channel_id=1, source_target_pairs={{0,1},{1,4},{4,5},{5,8},{8,9},{9,12},{12,13},{13,0},{2,3},{3,6},{6... | collective-permute-start | bytes 12296 | tf_op jit(solution)/shard_map/ppermute | solution.py:23
  101.3 4.8 %collective-permute-start.19 = (f32[4,1,256]{2,0,1:T(4,128)S(1)}, f32[4,1,256]{2,0,1:T(4,128)S(1)}, u32[]{:S(2)}, u32[]{:S(2)}) collective-permute-start(f32[4,1,256]{2,0,1:T(4,128)S(1)} %collective-permute-done.18), channel_id=1, source_target_pairs={{0,1},{1,4},{4,5},{5,8},{8,9},{9,12},{12,13},{13,0},{2,3},{3,6},{6... | collective-permute-start | bytes 12296 | tf_op jit(solution)/shard_map/ppermute | solution.py:23
  119.0 8.1 %collective-permute-start.25 = (f32[4,1,256]{2,0,1:T(4,128)S(1)}, f32[4,1,256]{2,0,1:T(4,128)S(1)}, u32[]{:S(2)}, u32[]{:S(2)}) collective-permute-start(f32[4,1,256]{2,0,1:T(4,128)S(1)} %get-tuple-element.145), channel_id=1, source_target_pairs={{0,1},{1,4},{4,5},{5,8},{8,9},{9,12},{12,13},{13,0},{2,3},{3,6},{6... | collective-permute-start | bytes 12296 | tf_op jit(solution)/shard_map/ppermute | solution.py:23
  119.9 37.8 %collective-permute-start.23 = (f32[2,1,32,256]{3,2,1,0:T(8,128)S(1)}, f32[2,1,32,256]{3,2,1,0:T(8,128)S(1)}, u32[]{:S(2)}, u32[]{:S(2)}) collective-permute-start(f32[2,1,32,256]{3,2,1,0:T(8,128)S(1)} %get-tuple-element.134), channel_id=1, source_target_pairs={{2,0},{3,1},{6,4},{7,5},{10,8},{11,9},{14,12},{15,13},{18,16},{19,... | collective-permute-start | bytes 196616 | tf_op jit(solution)/shard_map/ppermute | solution.py:37
  121.2 36.5 %collective-permute-start.22 = (f32[2,1,32,256]{3,2,1,0:T(8,128)S(1)}, f32[2,1,32,256]{3,2,1,0:T(8,128)S(1)}, u32[]{:S(2)}, u32[]{:S(2)}) collective-permute-start(f32[2,1,32,256]{3,2,1,0:T(8,128)S(1)} %get-tuple-element.133), channel_id=1, source_target_pairs={{0,2},{1,3},{4,6},{5,7},{8,10},{9,11},{12,14},{13,15},{16,18},{17,... | collective-permute-start | bytes 196616 | tf_op jit(solution)/shard_map/ppermute | solution.py:35
  127.1 4.9 %collective-permute-start.26 = (f32[4,1,256]{2,0,1:T(4,128)S(1)}, f32[4,1,256]{2,0,1:T(4,128)S(1)}, u32[]{:S(2)}, u32[]{:S(2)}) collective-permute-start(f32[4,1,256]{2,0,1:T(4,128)S(1)} %collective-permute-done.25), channel_id=1, source_target_pairs={{0,1},{1,4},{4,5},{5,8},{8,9},{9,12},{12,13},{13,0},{2,3},{3,6},{6... | collective-permute-start | bytes 12296 | tf_op jit(solution)/shard_map/ppermute | solution.py:23
  136.8 4.8 %collective-permute-start.28 = (f32[4,1,256]{2,0,1:T(4,128)S(1)}, f32[4,1,256]{2,0,1:T(4,128)S(1)}, u32[]{:S(2)}, u32[]{:S(2)}) collective-permute-start(f32[4,1,256]{2,0,1:T(4,128)S(1)} %collective-permute-done.27), channel_id=1, source_target_pairs={{0,1},{1,4},{4,5},{5,8},{8,9},{9,12},{12,13},{13,0},{2,3},{3,6},{6... | collective-permute-start | bytes 12296 | tf_op jit(solution)/shard_map/ppermute | solution.py:23
  158.0 61.7 %collective-permute-start.32 = (f32[2,6,1,256]{3,1,2,0:T(8,128)S(1)}, f32[2,6,1,256]{3,1,2,0:T(8,128)S(1)}, u32[]{:S(2)}, u32[]{:S(2)}) collective-permute-start(f32[2,6,1,256]{3,1,2,0:T(8,128)S(1)} %slice.192), channel_id=1, source_target_pairs={{0,1},{2,3},{4,5},{6,7},{8,9},{10,11},{12,13},{14,15},{16,17},{18,... | collective-permute-start | bytes 36872 | tf_op jit(solution)/shard_map/ppermute | solution.py:35
  160.2 13.8 %collective-permute-start.24 = (f32[2,6,1,256]{1,3,2,0:T(8,128)}, f32[2,6,1,256]{1,3,2,0:T(8,128)}, u32[]{:S(2)}, u32[]{:S(2)}) collective-permute-start(f32[2,6,1,256]{1,3,2,0:T(8,128)} %copy.292), channel_id=1, source_target_pairs={{1,0},{3,2},{5,4},{7,6},{9,8},{11,10},{13,12},{15,14},{17,16},{19,... | collective-permute-start | bytes 36872 | tf_op jit(solution)/shard_map/ppermute | solution.py:37
  170.6 40.4 %all-to-all-start.2 = ((f32[4,1,8192]{2,1,0:T(1,128)}), f32[4,1,8192]{2,1,0:T(1,128)S(1)}, u32[]{:S(2)}, u32[]{:S(2)}) async-start(f32[4,1,8192]{2,1,0:T(1,128)} %reshape.118), calls=%async_computation.2 | async-start | bytes 262144 | tf_op jit(solution)/shard_map/all_to_all | solution.py:154
  222.9 11.6 %collective-permute-start.36 = (f32[4,1,256]{2,0,1:T(4,128)S(1)}, f32[4,1,256]{2,0,1:T(4,128)S(1)}, u32[]{:S(2)}, u32[]{:S(2)}) collective-permute-start(f32[4,1,256]{2,0,1:T(4,128)S(1)} %get-tuple-element.143), channel_id=1, source_target_pairs={{0,1},{1,4},{4,5},{5,8},{8,9},{9,12},{12,13},{13,0},{2,3},{3,6},{6... | collective-permute-start | bytes 12296 | tf_op jit(solution)/shard_map/ppermute | solution.py:23
  223.0 52.1 %all-to-all-start.3 = ((f32[4,32,256]{2,0,1:T(4,128)}), f32[4,32,256]{2,0,1:T(4,128)S(1)}, u32[]{:S(2)}, u32[]{:S(2)}) async-start(f32[4,32,256]{2,0,1:T(4,128)} %multiply_subtract_fusion.1), calls=%async_computation.3 | async-start | bytes 262144 | tf_op jit(solution)/shard_map/all_to_all | solution.py:172
  227.3 37.8 %collective-permute-start.34 = (f32[2,1,32,256]{3,2,1,0:T(8,128)S(1)}, f32[2,1,32,256]{3,2,1,0:T(8,128)S(1)}, u32[]{:S(2)}, u32[]{:S(2)}) collective-permute-start(f32[2,1,32,256]{3,2,1,0:T(8,128)S(1)} %get-tuple-element.130), channel_id=1, source_target_pairs={{2,0},{3,1},{6,4},{7,5},{10,8},{11,9},{14,12},{15,13},{18,16},{19,... | collective-permute-start | bytes 196616 | tf_op jit(solution)/shard_map/ppermute | solution.py:37
  228.6 36.5 %collective-permute-start.33 = (f32[2,1,32,256]{3,2,1,0:T(8,128)S(1)}, f32[2,1,32,256]{3,2,1,0:T(8,128)S(1)}, u32[]{:S(2)}, u32[]{:S(2)}) collective-permute-start(f32[2,1,32,256]{3,2,1,0:T(8,128)S(1)} %get-tuple-element.129), channel_id=1, source_target_pairs={{0,2},{1,3},{4,6},{5,7},{8,10},{9,11},{12,14},{13,15},{16,18},{17,... | collective-permute-start | bytes 196616 | tf_op jit(solution)/shard_map/ppermute | solution.py:35
  234.5 5.5 %collective-permute-start.37 = (f32[4,1,256]{2,0,1:T(4,128)S(1)}, f32[4,1,256]{2,0,1:T(4,128)S(1)}, u32[]{:S(2)}, u32[]{:S(2)}) collective-permute-start(f32[4,1,256]{2,0,1:T(4,128)S(1)} %collective-permute-done.36), channel_id=1, source_target_pairs={{0,1},{1,4},{4,5},{5,8},{8,9},{9,12},{12,13},{13,0},{2,3},{3,6},{6... | collective-permute-start | bytes 12296 | tf_op jit(solution)/shard_map/ppermute | solution.py:23
  244.8 4.8 %collective-permute-start.39 = (f32[4,1,256]{2,0,1:T(4,128)S(1)}, f32[4,1,256]{2,0,1:T(4,128)S(1)}, u32[]{:S(2)}, u32[]{:S(2)}) collective-permute-start(f32[4,1,256]{2,0,1:T(4,128)S(1)} %collective-permute-done.38), channel_id=1, source_target_pairs={{0,1},{1,4},{4,5},{5,8},{8,9},{9,12},{12,13},{13,0},{2,3},{3,6},{6... | collective-permute-start | bytes 12296 | tf_op jit(solution)/shard_map/ppermute | solution.py:23
  254.5 4.8 %collective-permute-start.41 = (f32[4,1,256]{2,0,1:T(4,128)S(1)}, f32[4,1,256]{2,0,1:T(4,128)S(1)}, u32[]{:S(2)}, u32[]{:S(2)}) collective-permute-start(f32[4,1,256]{2,0,1:T(4,128)S(1)} %collective-permute-done.40), channel_id=1, source_target_pairs={{0,1},{1,4},{4,5},{5,8},{8,9},{9,12},{12,13},{13,0},{2,3},{3,6},{6... | collective-permute-start | bytes 12296 | tf_op jit(solution)/shard_map/ppermute | solution.py:23
  265.5 5.8 %collective-permute-start.43 = (f32[2,6,1,256]{3,1,2,0:T(8,128)S(1)}, f32[2,6,1,256]{3,1,2,0:T(8,128)S(1)}, u32[]{:S(2)}, u32[]{:S(2)}) collective-permute-start(f32[2,6,1,256]{3,1,2,0:T(8,128)S(1)} %slice.200), channel_id=1, source_target_pairs={{1,0},{3,2},{5,4},{7,6},{9,8},{11,10},{13,12},{15,14},{17,16},{19,... | collective-permute-start | bytes 36872 | tf_op jit(solution)/shard_map/ppermute | solution.py:37
  (32 other events, 376.1 us)
